TPU v7x, 128 devices: a whole 4x4x4 slice. The times are simulated.
128 devices in a mesh: gz: 8 (over z, x_hi), gx: 16 (over x_lo, y, core).
Axes of the slice: x: 4 (x_hi: 2, x_lo: 2; x = x_hi * 2 + x_lo), y: 4, z: 4, core: 2. Of those that a mesh axis runs over, the one named last changes fastest.
Arguments:
- source: float32 [16, 4096, 4096], P(None, 'gx', 'gz'), may hold values from -6 to 6
Outputs:
- spectrum: float32 [16, 2, 2048, 4096], P('gx', None, None, 'gz')
All inputs are finite; a program needn't handle non-finite values.
Results may differ from a plain program's by a relative error of at most 0.00007.
Values sent between devices are 32-bit elements; how exact they have to be, the bound alone decides.
A program may use at most 256 MiB of HBM per device.

v0:
```python
import math

import jax
import jax.numpy as jnp
from jax import lax
from jax.sharding import PartitionSpec as P


def fourier_tables(length, keep, total):
    rows = jnp.arange(length, dtype=jnp.int32)[:, None]
    cols = jnp.arange(keep, dtype=jnp.int32)[None, :]
    angle = 2.0 * math.pi / total * (rows * cols % total).astype(jnp.float32)
    return (jnp.cos(angle), jnp.sin(angle))


def product(form, left, right):
    return jnp.einsum(form, left, right, precision=lax.Precision.HIGHEST)


def span_transform(lines):
    planes, rows_here, length = lines.shape
    outer = length // 128
    wider = 2 * outer
    doubled = 2 * length
    blocks = lines.reshape(planes, rows_here, outer, 128)
    cos_first, sin_first = fourier_tables(outer, wider, wider)
    part_real = product("yxab,ac->yxcb", blocks, cos_first)
    part_imag = -product("yxab,ac->yxcb", blocks, sin_first)
    turn_cos, turn_sin = fourier_tables(wider, 128, doubled)
    turned_real = part_real * turn_cos + part_imag * turn_sin
    turned_imag = part_imag * turn_cos - part_real * turn_sin
    cos_second, sin_second = fourier_tables(128, 64, 128)
    whole_real = product("yxcb,bj->yxjc", turned_real, cos_second) + product(
        "yxcb,bj->yxjc", turned_imag, sin_second
    )
    whole_imag = product("yxcb,bj->yxjc", turned_imag, cos_second) - product(
        "yxcb,bj->yxjc", turned_real, sin_second
    )
    wave_index = (
        jnp.arange(64, dtype=jnp.int32)[:, None] * wider
        + jnp.arange(wider, dtype=jnp.int32)[None, :]
    )
    theta = math.pi / (2 * length) * wave_index.astype(jnp.float32)
    cosine = 2.0 * (jnp.cos(theta) * whole_real + jnp.sin(theta) * whole_imag)
    return cosine.reshape(planes, rows_here, length)


def periodic_transform(lines, factor):
    planes, length, depth = lines.shape
    outer = length // 128
    blocks = lines.reshape(planes, outer, 128, depth)
    cos_first, sin_first = fourier_tables(outer, outer, outer)
    part_real = product("yanz,ak->yknz", blocks, cos_first)
    part_imag = -product("yanz,ak->yknz", blocks, sin_first)
    turn_cos, turn_sin = fourier_tables(outer, 128, length)
    turn_cos = turn_cos[:, :, None]
    turn_sin = turn_sin[:, :, None]
    turned_real = part_real * turn_cos + part_imag * turn_sin
    turned_imag = part_imag * turn_cos - part_real * turn_sin
    cos_second, sin_second = fourier_tables(128, 64, 128)
    spec_real = product("yknz,nj->yjkz", turned_real, cos_second) + product(
        "yknz,nj->yjkz", turned_imag, sin_second
    )
    spec_imag = product("yknz,nj->yjkz", turned_imag, cos_second) - product(
        "yknz,nj->yjkz", turned_real, sin_second
    )
    half = length // 2
    spec_real = spec_real.reshape(planes, half, depth)
    spec_imag = spec_imag.reshape(planes, half, depth)
    signs = 1.0 - 2.0 * (jnp.arange(length, dtype=jnp.int32) % 2).astype(jnp.float32)
    highest = product("yxz,x->yz", lines, signs)
    spec_imag = jnp.concatenate([highest[:, None, :], spec_imag[:, 1:, :]], axis=1)
    return jnp.stack([spec_real * factor, spec_imag * factor], axis=1)


def local(source):
    span_groups = lax.axis_size("gz")
    plane_groups = lax.axis_size("gx")
    span_total = source.shape[2] * span_groups
    periodic_total = source.shape[1] * plane_groups
    factor = 1.0 / math.sqrt(span_total * periodic_total)
    cosine = span_transform(lax.all_to_all(source, "gz", split_axis=1, concat_axis=2, tiled=True))
    pencil = lax.all_to_all(
        lax.all_to_all(cosine, "gz", split_axis=2, concat_axis=1, tiled=True),
        "gx",
        split_axis=0,
        concat_axis=1,
        tiled=True,
    )
    return periodic_transform(pencil, factor)


def solution(mesh):
    placed = (P(None, "gx", "gz"),)
    return jax.shard_map(
        local, mesh=mesh, in_specs=placed, out_specs=P("gx", None, None, "gz"), check_vma=False
    )
```

profile of v0, /device:TPU:25, one launch (start us, length us, event | category | flops | bytes accessed | tf_op | source)
XLA Modules:
  0.0 864.7 jit_solution(7076593819783791691)
XLA Ops:
  0.0 11.6 %copy.26 = f32[16,256,512]{2,0,1:T(8,128)} copy(f32[16,256,512]{2,1,0:T(8,128)} %param.1) | data formatting | bytes 16777216 | tf_op args[0]
  11.6 7.9 all-to-all-start
  19.9 94.6 %all-to-all-done = f32[16,256,512]{2,0,1:T(8,128)} async-done(((f32[16,256,512]{2,0,1:T(8,128)}), f32[16,256,512]{2,0,1:T(8,128)}, u32[]{:S(2)}, u32[]{:S(2)}) %all-to-all-start) | async-done | bytes 8388640 | tf_op jit(solution)/shard_map/all_to_all | solution.py:82
  114.5 11.6 %copy.65 = f32[16,8,32,512]{3,1,2,0:T(8,128)} copy(f32[16,8,32,512]{3,0,2,1:T(8,128)} %bitcast.6) | data formatting | bytes 16777216 | tf_op jit(solution)/shard_map/all_to_all | solution.py:82
  126.2 9.0 %reshape.237 = f32[16,32,32,128]{3,2,1,0:T(8,128)} reshape(f32[16,32,8,512]{3,2,1,0:T(8,128)} %bitcast.88) | data formatting | bytes 16777216 | tf_op jit(solution)/shard_map/reshape | solution.py:25
  135.2 18.6 %fusion.66 = f32[64,16,32,128]{3,0,2,1:T(8,128)} fusion(f32[16,32,32,128]{3,2,1,0:T(8,128)} %reshape.237), kind=kOutput, calls=%fused_computation.88 | convolution fusion | flops 1610641408 | bytes 25165824 | tf_op jit(solution)/shard_map/yxab,ac->yxcb/dot_general | solution.py:17
  153.7 16.1 %fusion.68 = f32[64,16,32,128]{3,0,2,1:T(8,128)} fusion(f32[16,32,32,128]{3,2,1,0:T(8,128)S(1)} %copy-done), kind=kOutput, calls=%fused_computation.90 | convolution fusion | flops 1610641408 | bytes 25165824 | tf_op jit(solution)/shard_map/yxab,ac->yxcb/dot_general | solution.py:17
  169.9 69.7 %fusion.2 = f32[64,16,32,64]{3,0,2,1:T(8,128)} fusion(f32[64,16,32,128]{3,0,2,1:T(8,128)} %fusion.68, f32[64,16,32,128]{3,0,2,1:T(8,128)} %fusion.66, f32[64,128]{1,0:T(8,128)S(1)} %get-tuple-element.9, f32[64,128]{1,0:T(8,128)S(1)} %get-tuple-element.10), kind=kOutput, calls=%fused_computation.2 | convolution fusion | flops 3238117376 | bytes 42008576 | tf_op jit(solution)/shard_map/yxcb,bj->yxjc/dot_general | solution.py:17
  239.6 57.5 %fusion.4 = f32[64,16,32,64]{3,0,2,1:T(8,128)} fusion(f32[64,16,32,128]{3,0,2,1:T(8,128)} %fusion.68, f32[64,16,32,128]{3,0,2,1:T(8,128)} %fusion.66, f32[64,128]{1,0:T(8,128)S(1)} %get-tuple-element.9, f32[64,128]{1,0:T(8,128)S(1)} %get-tuple-element.10), kind=kOutput, calls=%fused_computation.4 | convolution fusion | flops 3238117376 | bytes 42008576 | tf_op jit(solution)/shard_map/yxcb,bj->yxjc/dot_general | solution.py:17
  297.0 57.8 %fusion = f32[64,16,32,64]{3,0,2,1:T(8,128)} fusion(f32[64,16,32,128]{3,0,2,1:T(8,128)} %fusion.68, f32[64,16,32,128]{3,0,2,1:T(8,128)} %fusion.66, f32[64,128]{1,0:T(8,128)S(1)} %get-tuple-element.9, f32[64,128]{1,0:T(8,128)S(1)} %get-tuple-element.10), kind=kOutput, calls=%fused_computation | convolution fusion | flops 3238117376 | bytes 42008576 | tf_op jit(solution)/shard_map/yxcb,bj->yxjc/dot_general | solution.py:17
  354.8 58.0 %multiply_bitcast_fusion = f32[16,32,64,64]{3,2,1,0:T(8,128)} fusion(f32[64,16,32,64]{3,0,2,1:T(8,128)} %fusion, f32[64,16,32,64]{3,0,2,1:T(8,128)} %fusion.4, f32[64,16,32,64]{3,0,2,1:T(8,128)} %fusion.2, f32[64,64]{1,0:T(8,128)S(1)} %get-tuple-element.8, f32[64,64]{1,0:T(8,128)S(1)} %get-tuple-element.7, f32[64,16,32,128]{3,0,2,1:T(8,128)} %fusion.68, ...), kind=kOutput, calls=%fused_computation.8 | convolution fusion | flops 3250700288 | bytes 67207168 | tf_op jit(solution)/shard_map/yxcb,bj->yxjc/dot_general | solution.py:17
  412.8 23.3 %copy.43 = f32[16,32,64,64]{1,0,3,2:T(8,128)} copy(f32[16,32,64,64]{3,2,1,0:T(8,128)} %multiply_bitcast_fusion) | data formatting | bytes 16777216 | tf_op jit(solution)/shard_map/reshape | solution.py:45
  436.1 20.5 %reshape.252 = f32[8,1,262144]{2,1,0:T(1,128)} reshape(f32[4096,16,32]{2,1,0:T(8,128)} %bitcast.85) | data formatting | bytes 16777216
  456.6 99.4 %all_to_all.42 = f32[8,1,262144]{2,1,0:T(1,128)} all-to-all(f32[8,1,262144]{2,1,0:T(1,128)} %reshape.252), channel_id=1, replica_groups=mesh['gz'=8,'gx'=16] {'gz'}, dimensions={0} | all-to-all | bytes 16777216 | tf_op jit(solution)/shard_map/all_to_all | solution.py:84
  556.0 0.6 broadcast.305
  556.6 26.6 %reduce = f32[8,262144]{1,0:T(8,128)} reduce(f32[8,1,262144]{2,1,0:T(1,128)} %all_to_all.42, f32[]{:T(128)} %broadcast.305), dimensions={1}, to_apply=%all_to_all.34.reduce_sub_computation | reduce | bytes 16777220 | tf_op jit(solution)/shard_map/all_to_all | solution.py:84
  583.2 25.3 %reshape.253 = f32[4096,16,32]{2,1,0:T(8,128)} reshape(f32[8,262144]{1,0:T(8,128)} %reduce) | data formatting | bytes 16777216
  608.4 21.7 %copy.30 = f32[16,8,32,512]{3,2,1,0:T(8,128)} copy(f32[16,8,32,512]{2,0,3,1:T(8,128)} %bitcast.86) | data formatting | bytes 16777216 | tf_op jit(solution)/shard_map/all_to_all | solution.py:84
  630.2 7.7 all-to-all-start.2
  638.2 128.1 %all-to-all-done.2 = f32[16,256,512]{2,1,0:T(8,128)} async-done(((f32[16,256,512]{2,1,0:T(8,128)}), f32[16,256,512]{2,1,0:T(8,128)}, u32[]{:S(2)}, u32[]{:S(2)}) %all-to-all-start.2) | async-done | bytes 8388640 | tf_op jit(solution)/shard_map/all_to_all | solution.py:83
  766.3 17.2 %fusion.18 = f32[32,128,512]{2,0,1:T(8,128)} fusion(f32[32,128,512]{2,1,0:T(8,128)} %bitcast.22), kind=kOutput, calls=%fused_computation.23 | convolution fusion | flops 805320704 | bytes 16777216 | tf_op jit(solution)/shard_map/yanz,ak->yknz/dot_general | solution.py:17
  783.5 20.9 %multiply_add_fusion.1 = (f32[32,128,512]{2,0,1:T(8,128)S(1)}, f32[32,128,512]{2,0,1:T(8,128)}) fusion(f32[32,128,512]{2,0,1:T(8,128)} %fusion.18, f32[32,128]{0,1:T(8,128)S(1)} %get-tuple-element.11, f32[32,128]{0,1:T(8,128)S(1)} %get-tuple-element.12, f32[32,128,512]{2,1,0:T(8,128)} %bitcast.22), kind=kOutput, calls=%fused_computation.14 | convolution fusion | flops 820000768 | bytes 33587200 | tf_op jit(solution)/shard_map/yanz,ak->yknz/dot_general | solution.py:17
  804.4 13.4 %fusion.12 = f32[64,32,512]{2,0,1:T(8,128)S(1)} fusion(f32[32,128,512]{2,0,1:T(8,128)} %get-tuple-element.6), kind=kOutput, calls=%fused_computation.17 | convolution fusion | flops 1610727424 | bytes 12582912 | tf_op jit(solution)/shard_map/yknz,nj->yjkz/dot_general | solution.py:17
  817.9 9.5 %fusion.10 = f32[64,32,512]{2,0,1:T(8,128)S(1)} fusion(f32[32,128,512]{2,0,1:T(8,128)S(1)} %copy-done.1), kind=kOutput, calls=%fused_computation.15 | convolution fusion | flops 1610727424 | bytes 12582912 | tf_op jit(solution)/shard_map/yknz,nj->yjkz/dot_general | solution.py:17
  827.3 10.1 %add_multiply_fusion = f32[64,32,512]{2,0,1:T(8,128)S(1)} fusion(f32[64,32,512]{2,0,1:T(8,128)S(1)} %fusion.12, f32[32,128,512]{2,0,1:T(8,128)S(1)} %get-tuple-element.5), kind=kOutput, calls=%fused_computation.29 | convolution fusion | flops 1612824576 | bytes 16777216 | tf_op jit(solution)/shard_map/yknz,nj->yjkz/dot_general | solution.py:17
  837.4 2.4 copy.35
  839.8 9.9 %fusion.24 = f32[64,32,512]{2,0,1:T(8,128)S(1)} fusion(f32[64,32,512]{2,0,1:T(8,128)S(1)} %fusion.10, f32[32,128,512]{2,0,1:T(8,128)S(1)} %get-tuple-element.5), kind=kOutput, calls=%fused_computation.30 | convolution fusion | flops 1611776000 | bytes 16777216 | tf_op jit(solution)/shard_map/yknz,nj->yjkz/dot_general | solution.py:17
  849.7 2.4 copy.38
  852.2 0.5 slice_bitcast_fusion
  852.7 6.9 convolution_bitcast_fusion
  859.6 0.5 maximum_multiply_fusion
  860.2 4.4 pad_maximum_fusion
  (9 shorter events, 0.6 us)
Async XLA Ops:
  11.6 102.9 %all-to-all-start = ((f32[16,256,512]{2,0,1:T(8,128)}), f32[16,256,512]{2,0,1:T(8,128)}, u32[]{:S(2)}, u32[]{:S(2)}) async-start(f32[16,256,512]{2,0,1:T(8,128)} %copy.26), calls=%async_computation | async-start | bytes 16777216 | tf_op jit(solution)/shard_map/all_to_all | solution.py:82
  135.2 18.6 %copy-start = (f32[16,32,32,128]{3,2,1,0:T(8,128)S(1)}, f32[16,32,32,128]{3,2,1,0:T(8,128)}, u32[]{:S(2)}) copy-start(f32[16,32,32,128]{3,2,1,0:T(8,128)} %reshape.237) | copy-start | bytes 25165828
  630.2 136.1 %all-to-all-start.2 = ((f32[16,256,512]{2,1,0:T(8,128)}), f32[16,256,512]{2,1,0:T(8,128)}, u32[]{:S(2)}, u32[]{:S(2)}) async-start(f32[16,256,512]{2,1,0:T(8,128)} %bitcast.87), calls=%async_computation.2 | async-start | bytes 16777216 | tf_op jit(solution)/shard_map/all_to_all | solution.py:83
  804.4 13.4 %copy-start.1 = (f32[32,128,512]{2,0,1:T(8,128)S(1)}, f32[32,128,512]{2,0,1:T(8,128)}, u32[]{:S(2)}) copy-start(f32[32,128,512]{2,0,1:T(8,128)} %get-tuple-element.6) | copy-start | bytes 25165828
where the time goes:
time: 871 us; the launch traced here: 865 us
  matrix products  366 us (42%)
  waiting for transfers between devices  223 us (26%)
  local copies, waits for them, and re-layouts  129 us (15%)
  blocking collectives  99.4 us (11%)
  other arithmetic  32.2 us (4%)
  starting transfers between devices  15.6 us (2%)
    dot_general x13, matrix products, product(): return jnp.einsum(form, left, right, precision=lax.Precision.HIGHEST)  366 us
    all_to_all x1, waiting for transfers between devices, local(): lax.all_to_all(lax.all_to_all(cosine, 'gz', split_axis=2, concat_axis=1,...  128 us
    all_to_all x1, blocking collectives, local(): lax.all_to_all(cosine, 'gz', split_axis=2, concat_axis=1, tiled=True)  99.4 us
    all_to_all x1, waiting for transfers between devices, local(): lax.all_to_all(source, 'gz', split_axis=1, concat_axis=2, tiled=True)  94.6 us
    unnamed x7, local copies, waits for them, and re-layouts  57.4 us
    all_to_all x1, other arithmetic, local(): lax.all_to_all(cosine, 'gz', split_axis=2, concat_axis=1, tiled=True)  26.6 us
    reshape x1, local copies, waits for them, and re-layouts, span_transform(): return cosine.reshape(planes, rows_here, length)  23.3 us
    all_to_all x2, local copies, waits for them, and re-layouts, local(): lax.all_to_all(cosine, 'gz', split_axis=2, concat_axis=1, tiled=True)  22.3 us
  transfers between devices with their start and end apart: 2, of which 2 were waited for; matrix products, arithmetic and copies ran while one was open for 0% of the time, Pallas kernels for 0%

commit v1 on v0

v1 whole, which is shorter than its diff:
```python
import functools
import math

import jax
import jax.numpy as jnp
import ml_dtypes
import numpy as np
from jax import lax
from jax.experimental import pallas as pl
from jax.experimental.pallas import tpu as pltpu
from jax.sharding import PartitionSpec as P

MESH = pl.DeviceIdType.MESH
BF16 = jnp.bfloat16
F32 = jnp.float32
CHUNKS = 4
STEP = 53


def halves(table):
    high = table.astype(np.float32).astype(ml_dtypes.bfloat16)
    low = (table - high.astype(np.float64)).astype(np.float32).astype(ml_dtypes.bfloat16)
    return np.stack([high, low])


def span_tables(length, groups):
    wide = length // groups
    turns = 2 * groups
    each = length // turns // groups
    offset = np.arange(wide)
    table = np.zeros((groups, 2, wide, groups // 2, 2, 2, each))
    for p in range(groups):
        for tile in range(groups // 2):
            for half in range(2):
                block = 2 * tile + (half ^ (p % 2))
                for which in range(2):
                    residue = (p, turns - p)[which] if p else (0, groups)[which]
                    k = residue + turns * (block * each + np.arange(each))
                    angle = math.pi / (2 * length) * (np.outer(2 * offset + 1, k) % (4 * length))
                    if p:
                        table[p, 0, :, tile, half, which] = 2 * np.cos(angle)
                        table[p, 1, :, tile, half, which] = 2 * np.sin(angle) * (1 - 2 * which)
                    else:
                        table[p, which, :, tile, half, which] = 2 * np.cos(angle)
    return halves(table.reshape(groups, 2 * wide, wide))


def order_tables(length, groups):
    wide = length // groups
    turns = 2 * groups
    each = wide // turns
    out = np.zeros((2, wide, wide), np.float32)
    for odd in range(2):
        row = 0
        for u in range(groups // 2):
            for half in range(2):
                p = 2 * u + (half ^ odd)
                for which in range(2):
                    residue = (p, turns - p)[which] if p else (0, groups)[which]
                    for j in range(each):
                        out[odd, row, j * turns + residue] = 1.0
                        row += 1
    return out.astype(ml_dtypes.bfloat16)


def periodic_tables(length, groups, factor):
    wide = length // groups
    each = wide // 2
    r = np.arange(wide)
    table = np.zeros((groups // 2, 2, 2, each, 2, wide))
    for p in range(groups // 2):
        for which in range(2):
            residue = (p, groups - p)[which] if p else (0, groups // 2)[which]
            q = residue + groups * np.arange(each)
            angle = 2 * math.pi / length * (np.outer(q, r) % length)
            cos, sin = np.cos(angle) * factor, np.sin(angle) * factor
            if p:
                sign = 1 - 2 * which
                table[p, which, 0, :, 0] = cos
                table[p, which, 0, :, 1] = sin * sign
                table[p, which, 1, :, 0] = -sin
                table[p, which, 1, :, 1] = cos * sign
            else:
                table[p, which, 0, :, which] = cos
                table[p, which, 1, :, which] = -sin
    table[0, 0, 1, 0, 0] = (1 - 2 * (r % 2)) * factor
    return halves(table.reshape(groups // 2, 2 * wide, 2 * wide))


def split(value):
    high = value.astype(BF16)
    return high, (value - high.astype(F32)).astype(BF16)


def sixteenths(even, odd):
    root = math.sqrt(0.5)

    def parts(s):
        plus, minus = root * (s[1] + s[3]), root * (s[1] - s[3])
        return plus, minus

    out = [None] * 8
    s = even[0::2]
    t = even[1::2]
    p0, q0 = (s[0] + s[2]) + (s[1] + s[3]), (t[0] + t[2]) + (t[1] + t[3])
    p4, q4 = (s[0] + s[2]) - (s[1] + s[3]), (t[0] + t[2]) - (t[1] + t[3])
    out[0] = (p0 + q0, p0 - q0)
    out[4] = (p4, -q4)
    p2 = (s[0] - s[2], s[3] - s[1])
    q2 = (t[0] - t[2], t[3] - t[1])
    w2 = (root * (q2[0] + q2[1]), root * (q2[1] - q2[0]))
    out[2] = (p2[0] + w2[0], p2[1] + w2[1])
    out[6] = (p2[0] - w2[0], w2[1] - p2[1])
    s = odd[0::2]
    t = odd[1::2]
    s_plus, s_minus = parts(s)
    t_plus, t_minus = parts(t)
    p1, p3 = (s[0] + s_minus, -s[2] - s_plus), (s[0] - s_minus, s[2] - s_plus)
    q1, q3 = (t[0] + t_minus, -t[2] - t_plus), (t[0] - t_minus, t[2] - t_plus)
    for k, pk, qk in ((1, p1, q1), (3, p3, q3)):
        c, d = math.cos(math.pi * k / 8), math.sin(math.pi * k / 8)
        wk = (c * qk[0] + d * qk[1], c * qk[1] - d * qk[0])
        out[k] = (pk[0] + wk[0], pk[1] + wk[1])
        out[8 - k] = (pk[0] - wk[0], wk[1] - pk[1])
    return out


def dot(left, right):
    return jnp.dot(left, right, preferred_element_type=F32)


def span_kernel(
    source, table, order, pencil, got, tables, orders, high, low, result, cosine,
    barrier_free, table_sem, own_sem, send1, recv1, send2, recv2, own2,
):
    gz, gx = lax.axis_index("gz"), lax.axis_index("gx")
    z, x_ring, y, core = gz // 2, (gz % 2) * 2 + gx // 8, (gx // 2) % 4, gx % 2
    groups, planes = got.shape[1], got.shape[2]
    peers = groups * planes - 1

    barrier = pltpu.get_barrier_semaphore()

    def greet_span(t, carry):
        pl.semaphore_signal(barrier, inc=1, device_id=((gz + t) % groups, gx), device_id_type=MESH)
        return carry

    def greet_planes(t, carry):
        pl.semaphore_signal(barrier, inc=1, device_id=(gz, (gx + t) % planes), device_id_type=MESH)
        return carry

    lax.fori_loop(1, groups, greet_span, 0)
    lax.fori_loop(1, planes, greet_planes, 0)
    pl.semaphore_wait(barrier, groups + planes - 2)

    def rows_for(group, c):
        return source.at[:, pl.ds(pl.multiple_of(group * (CHUNKS * 8) + c * 8, 8), 8), :]

    def scatter(i, carry):
        c, t = i // (groups - 1), i % (groups - 1) + 1
        to = ((z + t // 2) % 4) * 2 + (gz + t) % 2
        pltpu.make_async_remote_copy(
            src_ref=rows_for(to, c),
            dst_ref=got.at[c, gz],
            send_sem=send1,
            recv_sem=recv1.at[c],
            device_id=(to, gx),
            device_id_type=MESH,
        ).start()
        return carry

    lax.fori_loop(0, CHUNKS * (groups - 1), scatter, 0)
    for c in range(CHUNKS):
        pltpu.make_async_copy(rows_for(gz, c), got.at[c, gz], own_sem.at[c]).start()
    table_copy = pltpu.make_async_copy(table, tables, table_sem.at[0])
    order_copy = pltpu.make_async_copy(order, orders, table_sem.at[1])
    table_copy.start()
    order_copy.start()
    table_copy.wait()
    order_copy.wait()

    lower = lax.broadcasted_iota(jnp.int32, (planes * 8, 128), 1) < 64

    def chunk(c, carry):
        pltpu.make_async_copy(got.at[c, 0 : groups - 1], got.at[c, 0 : groups - 1], recv1.at[c]).wait()
        pltpu.make_async_copy(rows_for(gz, c), got.at[c, gz], own_sem.at[c]).wait()

        def first(i, inner):
            rows = pl.ds(pl.multiple_of(i * 16, 16), 16)
            for lane in range(4):
                lanes = pl.ds(lane * 128, 128)
                s = [got[c, b, pl.ds(i * 2, 2), :, lanes].reshape(16, 128) for b in range(groups)]
                for p, pair in enumerate(sixteenths(s, s)):
                    for part in range(2):
                        at = pl.ds(part * 512 + lane * 128, 128)
                        high[p, rows, at], low[p, rows, at] = split(pair[part])
            return inner

        lax.fori_loop(0, planes // 2, first, 0)

        def second(p, inner):
            value = dot(high[p], tables[0, p]) + dot(low[p], tables[0, p])
            result[p] = value + dot(high[p], tables[1, p])
            return inner

        lax.fori_loop(0, groups, second, 0)

        def third(t, inner):
            lanes = pl.ds(pl.multiple_of(t * 128, 128), 128)
            found = [result[p, :, lanes] for p in range(groups)]
            for odd in range(2):
                mixed = jnp.concatenate(
                    [
                        jnp.where(lower, found[2 * u + odd], found[2 * u + 1 - odd])
                        for u in range(groups // 2)
                    ],
                    axis=1,
                )
                top, rest = split(mixed)
                cosine[c, 2 * t + odd] = dot(top, orders[odd]) + dot(rest, orders[odd])
            return inner

        lax.fori_loop(0, groups // 2, third, 0)

        def send(t, inner):
            o = (t * STEP) % peers + 1
            to_x = (x_ring + (o // 8) % 4) % 4
            to_gz = ((z + o // 32) % 4) * 2 + to_x // 2
            to_gx = (to_x % 2) * 8 + ((y + (o // 2) % 4) % 4) * 2 + (core + o) % 2
            pltpu.make_async_remote_copy(
                src_ref=cosine.at[c, to_gz, pl.ds(pl.multiple_of(to_gx * 8, 8), 8), :],
                dst_ref=pencil.at[gx * groups + gz, c],
                send_sem=send2.at[c],
                recv_sem=recv2.at[c],
                device_id=(to_gz, to_gx),
                device_id_type=MESH,
            ).start()
            return inner

        lax.fori_loop(0, peers, send, 0)
        pltpu.make_async_copy(
            cosine.at[c, gz, pl.ds(pl.multiple_of(gx * 8, 8), 8), :],
            pencil.at[gx * groups + gz, c],
            own2.at[c],
        ).start()
        return carry

    lax.fori_loop(0, CHUNKS, chunk, 0)

    everything = got.at[:, 0 : groups - 1]
    pltpu.make_async_copy(everything, everything, send1).wait()
    for c in range(CHUNKS):
        arrived = pencil.at[0:peers, c]
        pltpu.make_async_copy(arrived, arrived, recv2.at[c]).wait()
        pltpu.make_async_copy(arrived, arrived, send2.at[c]).wait()
        pltpu.make_async_copy(
            cosine.at[c, gz, pl.ds(pl.multiple_of(gx * 8, 8), 8), :],
            pencil.at[gx * groups + gz, c],
            own2.at[c],
        ).wait()


def periodic_kernel(lines, table, out, high, low, stage, sems):
    pairs, wide = high.shape[0], lines.shape[1]
    tiles = lines.shape[2] // 128
    step = pl.program_id(0)

    def first(i, carry):
        rows = pl.ds(pl.multiple_of(i * 16, 16), 16)
        for lane in range(tiles):
            lanes = pl.ds(lane * 128, 128)
            s = [lines[g, rows, lanes] for g in range(2 * pairs)]
            even = [s[g] + s[g + pairs] for g in range(pairs)]
            odd = [s[g] - s[g + pairs] for g in range(pairs)]
            for p, pair in enumerate(sixteenths(even, odd)):
                for part in range(2):
                    at = pl.ds(pl.multiple_of(part * wide + i * 16, 16), 16)
                    high[p, at, lanes], low[p, at, lanes] = split(pair[part])
        return carry

    lax.fori_loop(0, wide // 16, first, 0)
    each = wide // 2
    for p in range(pairs):
        value = dot(table[0, p], high[p]) + dot(table[0, p], low[p])
        value = value + dot(table[1, p], high[p])
        for which in range(2):
            residue = (p, 2 * pairs - p)[which] if p else (0, pairs)[which]
            for part in range(2):
                piece = value[(2 * which + part) * each : (2 * which + part + 1) * each]
                for lane in range(tiles):
                    at = pl.ds(residue, each, stride=2 * pairs)
                    stage[step, lane, part, at, :] = piece[:, lane * 128 : lane * 128 + 128]

    def leave(at, lane):
        lanes = pl.ds(pl.multiple_of((at * tiles + lane) * 128, 128), 128)
        return pltpu.make_async_copy(stage.at[at, lane], out.at[0, :, :, lanes], sems.at[at, lane])

    for lane in range(tiles):
        leave(step, lane).start()

    @pl.when(step == pl.num_programs(0) - 1)
    def _():
        for at in range(stage.shape[0]):
            for lane in range(tiles):
                leave(at, lane).wait()


def local(source):
    groups, across = lax.axis_size("gz"), lax.axis_size("gx")
    planes, rows, wide = source.shape
    span_total, periodic_total = wide * groups, rows * across
    table = jnp.asarray(span_tables(span_total, groups))
    order = jnp.asarray(order_tables(span_total, groups))
    any_spec = pl.BlockSpec(memory_space=pl.ANY)
    lines = planes * 8
    pencil = pl.pallas_call(
        span_kernel,
        out_shape=jax.ShapeDtypeStruct((across * groups, CHUNKS, 8, wide), F32),
        in_specs=[any_spec] * 3,
        out_specs=any_spec,
        scratch_shapes=[
            pltpu.VMEM((CHUNKS, groups, planes, 8, wide), F32),
            pltpu.VMEM(table.shape, BF16),
            pltpu.VMEM(order.shape, BF16),
            pltpu.VMEM((groups, lines, 2 * wide), BF16),
            pltpu.VMEM((groups, lines, 2 * wide), BF16),
            pltpu.VMEM((groups, lines, wide), F32),
            pltpu.VMEM((CHUNKS, groups, lines, wide), F32),
            pltpu.SemaphoreType.REGULAR,
            pltpu.SemaphoreType.DMA((2,)),
            pltpu.SemaphoreType.DMA((CHUNKS,)),
            pltpu.SemaphoreType.DMA,
            pltpu.SemaphoreType.DMA((CHUNKS,)),
            pltpu.SemaphoreType.DMA((CHUNKS,)),
            pltpu.SemaphoreType.DMA((CHUNKS,)),
            pltpu.SemaphoreType.DMA((CHUNKS,)),
        ],
        compiler_params=pltpu.CompilerParams(
            collective_id=0, has_side_effects=True, vmem_limit_bytes=60 * 2**20
        ),
        name="span",
    )(source, table, order)
    factor = 1.0 / math.sqrt(span_total * periodic_total)
    periodic = jnp.asarray(periodic_tables(periodic_total, across, factor))
    block = 256
    return pl.pallas_call(
        periodic_kernel,
        grid=(wide // block,),
        out_shape=jax.ShapeDtypeStruct((1, 2, periodic_total // 2, wide), F32),
        in_specs=[
            pl.BlockSpec((across, rows, block), lambda i: (0, 0, i)),
            pl.BlockSpec(periodic.shape, lambda i: (0, 0, 0, 0), pipeline_mode=pl.Buffered(1)),
        ],
        out_specs=any_spec,
        scratch_shapes=[
            pltpu.VMEM((across // 2, 2 * rows, block), BF16),
            pltpu.VMEM((across // 2, 2 * rows, block), BF16),
            pltpu.VMEM((wide // block, block // 128, 2, periodic_total // 2, 128), F32),
            pltpu.SemaphoreType.DMA((wide // block, block // 128)),
        ],
        compiler_params=pltpu.CompilerParams(vmem_limit_bytes=60 * 2**20),
        name="periodic",
    )(pencil.reshape(across, rows, wide), periodic)


def solution(mesh):
    return jax.shard_map(
        local,
        mesh=mesh,
        in_specs=(P(None, "gx", "gz"),),
        out_specs=P("gx", None, None, "gz"),
        check_vma=False,
    )
```

time: 871 us -> 237 us (0.27)
  matrix products: 366 us -> 0 us
  Pallas kernels: 0 us -> 236 us
  waiting for transfers between devices: 223 us -> 0 us
  local copies, waits for them, and re-layouts: 129 us -> 0 us
  blocking collectives: 99.4 us -> 0 us
  other arithmetic: 32.2 us -> 0 us
  starting transfers between devices: 15.6 us -> 0 us
    dot_general x13 -> x0, matrix products: 366 us -> none  [product(): return jnp.einsum(form, left, right, precision=lax.Precision.HIGHEST)]
    pallas_call x0 -> x2, Pallas kernels: none -> 236 us  [the longest x1 218 us: local(): pl.pallas_call(span_kernel, out_shape=jax.ShapeDtypeStruct((across * grou...]
    all_to_all x2 -> x0, waiting for transfers between devices: 223 us -> none  [the longest x1 128 us: local(): lax.all_to_all(lax.all_to_all(cosine, 'gz', split_axis=2, concat_axis=1,...]
    all_to_all x1 -> x0, blocking collectives: 99.4 us -> none  [local(): lax.all_to_all(cosine, 'gz', split_axis=2, concat_axis=1, tiled=True)]
    unnamed x7 -> x0, local copies, waits for them, and re-layouts: 57.4 us -> none
    all_to_all x3 -> x0, local copies, waits for them, and re-layouts: 33.9 us -> none  [the longest x2 22.3 us: local(): lax.all_to_all(cosine, 'gz', split_axis=2, concat_axis=1, tiled=True)]
    reshape x2 -> x0, local copies, waits for them, and re-layouts: 32.3 us -> none  [the longest x1 23.3 us: span_transform(): return cosine.reshape(planes, rows_here, length)]
    all_to_all x1 -> x0, other arithmetic: 26.6 us -> none  [local(): lax.all_to_all(cosine, 'gz', split_axis=2, concat_axis=1, tiled=True)]
  transfers between devices with their start and end apart: 2 -> 0, of which waited for: 2 -> 0; matrix products, arithmetic and copies ran while one was open for 0% -> 0% of each run, Pallas kernels for 0% -> 0%
where the time goes in v1:
time: 237 us
  Pallas kernels  236 us (100%)
    pallas_call x1, Pallas kernels, local(): pl.pallas_call(span_kernel, out_shape=jax.ShapeDtypeStruct((across * grou...  218 us
    pallas_call x1, Pallas kernels, local(): pl.pallas_call(periodic_kernel, grid=(wide // block,), out_shape=jax.Shap...  18.4 us

profile of v1, /device:TPU:25, one launch (start us, length us, event | category | flops | bytes accessed | tf_op | source)
XLA Modules:
  0.0 236.5 jit_solution(17826659052642952080)
XLA Ops:
  0.0 218.1 %span.1 = f32[128,4,8,512]{3,2,1,0:T(8,128)} custom-call(f32[16,256,512]{2,1,0:T(8,128)} %source.1, bf16[2,8,1024,512]{3,2,1,0:T(8,128)(2,1)} %constant.6.clone.table, bf16[2,512,512]{2,1,0:T(8,128)(2,1)} %constant.7.clone.order), custom_call_target="tpu_custom_call" | custom-call | tf_op jit(solution)/shard_map/span/pallas_call | solution.py:315
  218.1 18.4 %periodic.1 = f32[1,2,2048,512]{3,2,1,0:T(8,128)} custom-call(f32[16,256,512]{2,1,0:T(8,128)} %bitcast.1, bf16[2,8,512,512]{3,2,1,0:T(8,128)(2,1)} %constant.8.clone.table), custom_call_target="tpu_custom_call" | custom-call | tf_op jit(solution)/shard_map/periodic/pallas_call | solution.py:345

commit v2 on v1

--- a/solution.py
+++ b/solution.py
@@ -1,4 +1,3 @@
-import functools
 import math
 
 import jax
@@ -14,7 +13,7 @@
 BF16 = jnp.bfloat16
 F32 = jnp.float32
 CHUNKS = 4
-STEP = 53
+STEP = 41
 
 
 def halves(table):
@@ -63,10 +62,11 @@
     return out.astype(ml_dtypes.bfloat16)
 
 
-def periodic_tables(length, groups, factor):
+def periodic_tables(length, groups, spans, factor):
     wide = length // groups
     each = wide // 2
-    r = np.arange(wide)
+    rest = wide // spans // CHUNKS
+    r = np.arange(wide).reshape(spans, CHUNKS, rest).transpose(1, 0, 2).reshape(-1)
     table = np.zeros((groups // 2, 2, 2, each, 2, wide))
     for p in range(groups // 2):
         for which in range(2):
@@ -84,7 +84,8 @@
                 table[p, which, 0, :, which] = cos
                 table[p, which, 1, :, which] = -sin
     table[0, 0, 1, 0, 0] = (1 - 2 * (r % 2)) * factor
-    return halves(table.reshape(groups // 2, 2 * wide, 2 * wide))
+    high, low = halves(table.reshape(groups // 2, 2 * wide, 2 * wide))
+    return np.concatenate([high, low], axis=1)
 
 
 def split(value):
@@ -129,15 +130,15 @@
     return jnp.dot(left, right, preferred_element_type=F32)
 
 
-def span_kernel(
-    source, table, order, pencil, got, tables, orders, high, low, result, cosine,
-    barrier_free, table_sem, own_sem, send1, recv1, send2, recv2, own2,
+def kernel(
+    source, span_table, order_table, periodic_table, out, got, tables, orders, high, low, result, cosine, pencil, stage,
+    table_sem, own_sem, send1, recv1, send2, recv2, own2, out_sem,
 ):
     gz, gx = lax.axis_index("gz"), lax.axis_index("gx")
     z, x_ring, y, core = gz // 2, (gz % 2) * 2 + gx // 8, (gx // 2) % 4, gx % 2
-    groups, planes = got.shape[1], got.shape[2]
+    groups, planes, wide = got.shape[1], got.shape[2], got.shape[4]
     peers = groups * planes - 1
-
+    last = CHUNKS - 1
     barrier = pltpu.get_barrier_semaphore()
 
     def greet_span(t, carry):
@@ -171,8 +172,8 @@
     lax.fori_loop(0, CHUNKS * (groups - 1), scatter, 0)
     for c in range(CHUNKS):
         pltpu.make_async_copy(rows_for(gz, c), got.at[c, gz], own_sem.at[c]).start()
-    table_copy = pltpu.make_async_copy(table, tables, table_sem.at[0])
-    order_copy = pltpu.make_async_copy(order, orders, table_sem.at[1])
+    table_copy = pltpu.make_async_copy(span_table, tables, table_sem.at[0])
+    order_copy = pltpu.make_async_copy(order_table, orders, table_sem.at[1])
     table_copy.start()
     order_copy.start()
     table_copy.wait()
@@ -180,18 +181,19 @@
 
     lower = lax.broadcasted_iota(jnp.int32, (planes * 8, 128), 1) < 64
 
-    def chunk(c, carry):
+    def take(c):
         pltpu.make_async_copy(got.at[c, 0 : groups - 1], got.at[c, 0 : groups - 1], recv1.at[c]).wait()
         pltpu.make_async_copy(rows_for(gz, c), got.at[c, gz], own_sem.at[c]).wait()
 
+    def span_chunk(c):
         def first(i, inner):
             rows = pl.ds(pl.multiple_of(i * 16, 16), 16)
-            for lane in range(4):
+            for lane in range(wide // 128):
                 lanes = pl.ds(lane * 128, 128)
                 s = [got[c, b, pl.ds(i * 2, 2), :, lanes].reshape(16, 128) for b in range(groups)]
                 for p, pair in enumerate(sixteenths(s, s)):
                     for part in range(2):
-                        at = pl.ds(part * 512 + lane * 128, 128)
+                        at = pl.ds(part * wide + lane * 128, 128)
                         high[p, rows, at], low[p, rows, at] = split(pair[part])
             return inner
 
@@ -221,101 +223,131 @@
 
         lax.fori_loop(0, groups // 2, third, 0)
 
-        def send(t, inner):
+    def mine(c, lanes):
+        return pltpu.make_async_copy(
+            cosine.at[c, gz, pl.ds(pl.multiple_of(gx * 8, 8), 8), lanes],
+            pencil.at[gx * groups + gz, c, :, lanes],
+            own2.at[c],
+        )
+
+    def send(c, slot, lanes):
+        def one(t, inner):
             o = (t * STEP) % peers + 1
             to_x = (x_ring + (o // 8) % 4) % 4
             to_gz = ((z + o // 32) % 4) * 2 + to_x // 2
             to_gx = (to_x % 2) * 8 + ((y + (o // 2) % 4) % 4) * 2 + (core + o) % 2
             pltpu.make_async_remote_copy(
-                src_ref=cosine.at[c, to_gz, pl.ds(pl.multiple_of(to_gx * 8, 8), 8), :],
-                dst_ref=pencil.at[gx * groups + gz, c],
-                send_sem=send2.at[c],
-                recv_sem=recv2.at[c],
+                src_ref=cosine.at[c, to_gz, pl.ds(pl.multiple_of(to_gx * 8, 8), 8), lanes],
+                dst_ref=pencil.at[gx * groups + gz, c, :, lanes],
+                send_sem=send2.at[slot],
+                recv_sem=recv2.at[slot],
                 device_id=(to_gz, to_gx),
                 device_id_type=MESH,
             ).start()
             return inner
 
-        lax.fori_loop(0, peers, send, 0)
-        pltpu.make_async_copy(
-            cosine.at[c, gz, pl.ds(pl.multiple_of(gx * 8, 8), 8), :],
-            pencil.at[gx * groups + gz, c],
-            own2.at[c],
-        ).start()
+        lax.fori_loop(0, peers, one, 0)
+
+    every = pl.ds(0, wide)
+    block = wide // 2
+    sides = [pl.ds(h * block, block) for h in range(2)]
+
+    def early(c, carry):
+        take(c)
+        span_chunk(c)
+        mine(c, every).start()
         return carry
 
-    lax.fori_loop(0, CHUNKS, chunk, 0)
+    lax.fori_loop(0, last, early, 0)
+    send(0, 0, every)
+    take(last)
+    send(1, 1, every)
+    span_chunk(last)
+    mine(last, every).start()
+    for c in range(2, last):
+        send(c, c, every)
+    for h in range(2):
+        send(last, last + h, sides[h])
+
+    periodic_copy = pltpu.make_async_copy(periodic_table, tables.at[0], table_sem.at[0])
+    periodic_copy.start()
+    pairs = planes // 2
+    each = wide // 4
+
+    def fold(c, tiles):
+        def step(i, carry):
+            for lane in tiles:
+                lanes = pl.ds(lane * 128, 128)
+                s = [pencil[pl.ds(g * groups + i * 2, 2), c, :, lanes].reshape(16, 128) for g in range(planes)]
+                even = [s[g] + s[g + pairs] for g in range(pairs)]
+                odd = [s[g] - s[g + pairs] for g in range(pairs)]
+                for p, pair in enumerate(sixteenths(even, odd)):
+                    for part in range(2):
+                        at = part * (wide // 2) + c * (groups * 8) + i * 16
+                        top = pl.ds(pl.multiple_of(at, 16), 16)
+                        rest = pl.ds(pl.multiple_of(at + wide, 16), 16)
+                        tables[1, p, top, lanes], tables[1, p, rest, lanes] = split(pair[part])
+            return carry
+
+        lax.fori_loop(0, groups // 2, step, 0)
+
+    def arrived(c, slot, lanes):
+        view = pencil.at[0:peers, c, :, lanes]
+        return pltpu.make_async_copy(view, view, recv2.at[slot])
+
+    def leave(lane):
+        lanes = pl.ds(lane * 128, 128)
+        return pltpu.make_async_copy(stage.at[lane], out.at[0, :, :, lanes], out_sem.at[lane])
+
+    for c in range(last):
+        arrived(c, c, every).wait()
+        mine(c, every).wait()
+        fold(c, range(wide // 128))
+    mine(last, every).wait()
+    periodic_copy.wait()
+    for h in range(2):
+        arrived(last, last + h, sides[h]).wait()
+        tiles = range(h * block // 128, (h + 1) * block // 128)
+        fold(last, tiles)
+        for p in range(pairs):
+            table_high, table_low = tables[0, p, 0:wide, :], tables[0, p, wide : 2 * wide, :]
+            line_high, line_low = tables[1, p, 0:wide, sides[h]], tables[1, p, wide : 2 * wide, sides[h]]
+            value = dot(table_high, line_high) + dot(table_high, line_low) + dot(table_low, line_high)
+            for which in range(2):
+                residue = (p, planes - p)[which] if p else (0, pairs)[which]
+                for part in range(2):
+                    piece = value[(2 * which + part) * each : (2 * which + part + 1) * each]
+                    for n, lane in enumerate(tiles):
+                        at = pl.ds(residue, each, stride=planes)
+                        stage[lane, part, at, :] = piece[:, n * 128 : n * 128 + 128]
+        for lane in tiles:
+            leave(lane).start()
 
     everything = got.at[:, 0 : groups - 1]
     pltpu.make_async_copy(everything, everything, send1).wait()
-    for c in range(CHUNKS):
-        arrived = pencil.at[0:peers, c]
-        pltpu.make_async_copy(arrived, arrived, recv2.at[c]).wait()
-        pltpu.make_async_copy(arrived, arrived, send2.at[c]).wait()
-        pltpu.make_async_copy(
-            cosine.at[c, gz, pl.ds(pl.multiple_of(gx * 8, 8), 8), :],
-            pencil.at[gx * groups + gz, c],
-            own2.at[c],
-        ).wait()
-
-
-def periodic_kernel(lines, table, out, high, low, stage, sems):
-    pairs, wide = high.shape[0], lines.shape[1]
-    tiles = lines.shape[2] // 128
-    step = pl.program_id(0)
-
-    def first(i, carry):
-        rows = pl.ds(pl.multiple_of(i * 16, 16), 16)
-        for lane in range(tiles):
-            lanes = pl.ds(lane * 128, 128)
-            s = [lines[g, rows, lanes] for g in range(2 * pairs)]
-            even = [s[g] + s[g + pairs] for g in range(pairs)]
-            odd = [s[g] - s[g + pairs] for g in range(pairs)]
-            for p, pair in enumerate(sixteenths(even, odd)):
-                for part in range(2):
-                    at = pl.ds(pl.multiple_of(part * wide + i * 16, 16), 16)
-                    high[p, at, lanes], low[p, at, lanes] = split(pair[part])
-        return carry
-
-    lax.fori_loop(0, wide // 16, first, 0)
-    each = wide // 2
-    for p in range(pairs):
-        value = dot(table[0, p], high[p]) + dot(table[0, p], low[p])
-        value = value + dot(table[1, p], high[p])
-        for which in range(2):
-            residue = (p, 2 * pairs - p)[which] if p else (0, pairs)[which]
-            for part in range(2):
-                piece = value[(2 * which + part) * each : (2 * which + part + 1) * each]
-                for lane in range(tiles):
-                    at = pl.ds(residue, each, stride=2 * pairs)
-                    stage[step, lane, part, at, :] = piece[:, lane * 128 : lane * 128 + 128]
-
-    def leave(at, lane):
-        lanes = pl.ds(pl.multiple_of((at * tiles + lane) * 128, 128), 128)
-        return pltpu.make_async_copy(stage.at[at, lane], out.at[0, :, :, lanes], sems.at[at, lane])
-
-    for lane in range(tiles):
-        leave(step, lane).start()
-
-    @pl.when(step == pl.num_programs(0) - 1)
-    def _():
-        for at in range(stage.shape[0]):
-            for lane in range(tiles):
-                leave(at, lane).wait()
+    for slot in range(CHUNKS + 1):
+        lanes = every if slot < last else sides[slot - last]
+        view = pencil.at[0:peers, min(slot, last), :, lanes]
+        pltpu.make_async_copy(view, view, send2.at[slot]).wait()
+    for lane in range(wide // 128):
+        leave(lane).wait()
 
 
 def local(source):
     groups, across = lax.axis_size("gz"), lax.axis_size("gx")
     planes, rows, wide = source.shape
     span_total, periodic_total = wide * groups, rows * across
+    factor = 1.0 / math.sqrt(span_total * periodic_total)
     table = jnp.asarray(span_tables(span_total, groups))
     order = jnp.asarray(order_tables(span_total, groups))
+    periodic = jnp.asarray(periodic_tables(periodic_total, across, groups, factor))
     any_spec = pl.BlockSpec(memory_space=pl.ANY)
     lines = planes * 8
-    pencil = pl.pallas_call(
-        span_kernel,
-        out_shape=jax.ShapeDtypeStruct((across * groups, CHUNKS, 8, wide), F32),
-        in_specs=[any_spec] * 3,
+    half = periodic_total // 2
+    return pl.pallas_call(
+        kernel,
+        out_shape=jax.ShapeDtypeStruct((1, 2, half, wide), F32),
+        in_specs=[any_spec] * 4,
         out_specs=any_spec,
         scratch_shapes=[
             pltpu.VMEM((CHUNKS, groups, planes, 8, wide), F32),
@@ -325,41 +357,22 @@
             pltpu.VMEM((groups, lines, 2 * wide), BF16),
             pltpu.VMEM((groups, lines, wide), F32),
             pltpu.VMEM((CHUNKS, groups, lines, wide), F32),
-            pltpu.SemaphoreType.REGULAR,
+            pltpu.VMEM((across * groups, CHUNKS, 8, wide), F32),
+            pltpu.VMEM((wide // 128, 2, half, 128), F32),
             pltpu.SemaphoreType.DMA((2,)),
             pltpu.SemaphoreType.DMA((CHUNKS,)),
             pltpu.SemaphoreType.DMA,
             pltpu.SemaphoreType.DMA((CHUNKS,)),
+            pltpu.SemaphoreType.DMA((CHUNKS + 1,)),
+            pltpu.SemaphoreType.DMA((CHUNKS + 1,)),
             pltpu.SemaphoreType.DMA((CHUNKS,)),
-            pltpu.SemaphoreType.DMA((CHUNKS,)),
-            pltpu.SemaphoreType.DMA((CHUNKS,)),
+            pltpu.SemaphoreType.DMA((wide // 128,)),
         ],
         compiler_params=pltpu.CompilerParams(
-            collective_id=0, has_side_effects=True, vmem_limit_bytes=60 * 2**20
+            collective_id=0, has_side_effects=True, vmem_limit_bytes=62 * 2**20
         ),
-        name="span",
-    )(source, table, order)
-    factor = 1.0 / math.sqrt(span_total * periodic_total)
-    periodic = jnp.asarray(periodic_tables(periodic_total, across, factor))
-    block = 256
-    return pl.pallas_call(
-        periodic_kernel,
-        grid=(wide // block,),
-        out_shape=jax.ShapeDtypeStruct((1, 2, periodic_total // 2, wide), F32),
-        in_specs=[
-            pl.BlockSpec((across, rows, block), lambda i: (0, 0, i)),
-            pl.BlockSpec(periodic.shape, lambda i: (0, 0, 0, 0), pipeline_mode=pl.Buffered(1)),
-        ],
-        out_specs=any_spec,
-        scratch_shapes=[
-            pltpu.VMEM((across // 2, 2 * rows, block), BF16),
-            pltpu.VMEM((across // 2, 2 * rows, block), BF16),
-            pltpu.VMEM((wide // block, block // 128, 2, periodic_total // 2, 128), F32),
-            pltpu.SemaphoreType.DMA((wide // block, block // 128)),
-        ],
-        compiler_params=pltpu.CompilerParams(vmem_limit_bytes=60 * 2**20),
-        name="periodic",
-    )(pencil.reshape(across, rows, wide), periodic)
+        name="transform",
+    )(source, table, order, periodic)
 
 
 def solution(mesh):

time: 237 us -> 217 us (0.916)
  Pallas kernels: 236 us -> 207 us
  local copies, waits for them, and re-layouts: 0 us -> 7.76 us
    pallas_call x2 -> x1, Pallas kernels: 236 us -> 207 us  [local(): pl.pallas_call(kernel, out_shape=jax.ShapeDtypeStruct((1, 2, half, wide),...]
    unnamed x0 -> x1, local copies, waits for them, and re-layouts: none -> 7.76 us
where the time goes in v2:
time: 217 us; the launch traced here: 215 us
  Pallas kernels  207 us (95%)
  local copies, waits for them, and re-layouts  7.76 us (4%)
    pallas_call x1, Pallas kernels, local(): pl.pallas_call(kernel, out_shape=jax.ShapeDtypeStruct((1, 2, half, wide),...  207 us
    unnamed x1, local copies, waits for them, and re-layouts  7.76 us

profile of v2, /device:TPU:25, one launch (start us, length us, event | category | flops | bytes accessed | tf_op | source)
XLA Modules:
  0.0 214.7 jit_solution(12454492832039304800)
XLA Ops:
  0.0 206.9 %transform.1 = f32[1,2,2048,512]{3,2,1,0:T(8,128)} custom-call(f32[16,256,512]{2,1,0:T(8,128)} %source.1, bf16[2,8,1024,512]{3,2,1,0:T(8,128)(2,1)} %constant.6.clone.span_table, bf16[2,512,512]{2,1,0:T(8,128)(2,1)} %constant.7.clone.order_table, bf16[8,1024,512]{2,1,0:T(8,128)(2,1)} %constant.8.clone.periodic_table), custom_call_target="tpu_custom_call" | custom-call | tf_op jit(solution)/shard_map/transform/pallas_call | solution.py:347
  206.9 7.8 %copy.6 = f32[1,2,2048,512]{3,2,1,0:T(8,128)} copy(f32[1,2,2048,512]{3,2,1,0:T(8,128)} %transform.1) | data formatting | bytes 16777216

commit v3 on v2

--- a/solution.py
+++ b/solution.py
@@ -84,7 +84,10 @@
                 table[p, which, 0, :, which] = cos
                 table[p, which, 1, :, which] = -sin
     table[0, 0, 1, 0, 0] = (1 - 2 * (r % 2)) * factor
-    high, low = halves(table.reshape(groups // 2, 2 * wide, 2 * wide))
+    cut = wide - wide // CHUNKS
+    table = table.reshape(groups // 2, 2 * wide, 2, wide)
+    table = [t.reshape(groups // 2, 2 * wide, -1) for t in (table[..., :cut], table[..., cut:])]
+    high, low = halves(np.concatenate(table, axis=-1))
     return np.concatenate([high, low], axis=1)
 
 
@@ -131,8 +134,8 @@
 
 
 def kernel(
-    source, span_table, order_table, periodic_table, out, got, tables, orders, high, low, result, cosine, pencil, stage,
-    table_sem, own_sem, send1, recv1, send2, recv2, own2, out_sem,
+    source, span_table, order_table, periodic_table, stage, got, tables, orders, high, low, result, cosine, pencil,
+    table_sem, own_sem, send1, recv1, send2, recv2, own2,
 ):
     gz, gx = lax.axis_index("gz"), lax.axis_index("gx")
     z, x_ring, y, core = gz // 2, (gz % 2) * 2 + gx // 8, (gx // 2) % 4, gx % 2
@@ -273,6 +276,7 @@
     periodic_copy.start()
     pairs = planes // 2
     each = wide // 4
+    main = 2 * last * groups * 8
 
     def fold(c, tiles):
         def step(i, carry):
@@ -283,7 +287,7 @@
                 odd = [s[g] - s[g + pairs] for g in range(pairs)]
                 for p, pair in enumerate(sixteenths(even, odd)):
                     for part in range(2):
-                        at = part * (wide // 2) + c * (groups * 8) + i * 16
+                        at = part * (groups * 8) + (main if c == last else part * (main // 2 - groups * 8) + c * (groups * 8)) + i * 16
                         top = pl.ds(pl.multiple_of(at, 16), 16)
                         rest = pl.ds(pl.multiple_of(at + wide, 16), 16)
                         tables[1, p, top, lanes], tables[1, p, rest, lanes] = split(pair[part])
@@ -295,33 +299,44 @@
         view = pencil.at[0:peers, c, :, lanes]
         return pltpu.make_async_copy(view, view, recv2.at[slot])
 
-    def leave(lane):
-        lanes = pl.ds(lane * 128, 128)
-        return pltpu.make_async_copy(stage.at[lane], out.at[0, :, :, lanes], out_sem.at[lane])
-
     for c in range(last):
         arrived(c, c, every).wait()
         mine(c, every).wait()
         fold(c, range(wide // 128))
+    periodic_copy.wait()
+
+    def gather(p, carry):
+        table_high, table_low = tables[0, p, 0:wide, 0:main], tables[0, p, wide : 2 * wide, 0:main]
+        for side in sides:
+            line_high, line_low = tables[1, p, 0:main, side], tables[1, p, wide : wide + main, side]
+            value = dot(table_high, line_high) + dot(table_high, line_low) + dot(table_low, line_high)
+            for k in range(4):
+                piece = value[k * each : (k + 1) * each].reshape(planes, 8, block)
+                got[p // 2, (p % 2) * 4 + k, :, :, side] = piece
+        return carry
+
+    lax.fori_loop(0, pairs, gather, 0)
     mine(last, every).wait()
-    periodic_copy.wait()
     for h in range(2):
         arrived(last, last + h, sides[h]).wait()
         tiles = range(h * block // 128, (h + 1) * block // 128)
         fold(last, tiles)
         for p in range(pairs):
-            table_high, table_low = tables[0, p, 0:wide, :], tables[0, p, wide : 2 * wide, :]
-            line_high, line_low = tables[1, p, 0:wide, sides[h]], tables[1, p, wide : 2 * wide, sides[h]]
-            value = dot(table_high, line_high) + dot(table_high, line_low) + dot(table_low, line_high)
+            table_high, table_low = tables[0, p, 0:wide, main:wide], tables[0, p, wide : 2 * wide, main:wide]
+            line_high, line_low = tables[1, p, main:wide, sides[h]], tables[1, p, wide + main : 2 * wide, sides[h]]
+            value = dot(
+                jnp.concatenate([table_high, table_high], axis=1),
+                jnp.concatenate([line_high, line_low], axis=0),
+            ) + dot(table_low, line_high)
             for which in range(2):
                 residue = (p, planes - p)[which] if p else (0, pairs)[which]
                 for part in range(2):
-                    piece = value[(2 * which + part) * each : (2 * which + part + 1) * each]
+                    k = 2 * which + part
+                    before = got[p // 2, (p % 2) * 4 + k, :, :, sides[h]].reshape(each, block)
+                    piece = value[k * each : (k + 1) * each] + before
                     for n, lane in enumerate(tiles):
                         at = pl.ds(residue, each, stride=planes)
                         stage[lane, part, at, :] = piece[:, n * 128 : n * 128 + 128]
-        for lane in tiles:
-            leave(lane).start()
 
     everything = got.at[:, 0 : groups - 1]
     pltpu.make_async_copy(everything, everything, send1).wait()
@@ -329,8 +344,20 @@
         lanes = every if slot < last else sides[slot - last]
         view = pencil.at[0:peers, min(slot, last), :, lanes]
         pltpu.make_async_copy(view, view, send2.at[slot]).wait()
-    for lane in range(wide // 128):
-        leave(lane).wait()
+
+
+def place(tiles, out, sems):
+    copies = [
+        pltpu.make_async_copy(
+            tiles.at[lane, part], out.at[0, part, :, pl.ds(lane * 128, 128)], sems.at[lane, part]
+        )
+        for lane in range(tiles.shape[0])
+        for part in range(2)
+    ]
+    for copy in copies:
+        copy.start()
+    for copy in copies:
+        copy.wait()
 
 
 def local(source):
@@ -344,11 +371,11 @@
     any_spec = pl.BlockSpec(memory_space=pl.ANY)
     lines = planes * 8
     half = periodic_total // 2
-    return pl.pallas_call(
+    tiles = pl.pallas_call(
         kernel,
-        out_shape=jax.ShapeDtypeStruct((1, 2, half, wide), F32),
+        out_shape=pltpu.VMEM((wide // 128, 2, half, 128), F32),
         in_specs=[any_spec] * 4,
-        out_specs=any_spec,
+        out_specs=pl.BlockSpec(memory_space=pltpu.VMEM),
         scratch_shapes=[
             pltpu.VMEM((CHUNKS, groups, planes, 8, wide), F32),
             pltpu.VMEM(table.shape, BF16),
@@ -358,7 +385,6 @@
             pltpu.VMEM((groups, lines, wide), F32),
             pltpu.VMEM((CHUNKS, groups, lines, wide), F32),
             pltpu.VMEM((across * groups, CHUNKS, 8, wide), F32),
-            pltpu.VMEM((wide // 128, 2, half, 128), F32),
             pltpu.SemaphoreType.DMA((2,)),
             pltpu.SemaphoreType.DMA((CHUNKS,)),
             pltpu.SemaphoreType.DMA,
@@ -366,13 +392,21 @@
             pltpu.SemaphoreType.DMA((CHUNKS + 1,)),
             pltpu.SemaphoreType.DMA((CHUNKS + 1,)),
             pltpu.SemaphoreType.DMA((CHUNKS,)),
-            pltpu.SemaphoreType.DMA((wide // 128,)),
         ],
         compiler_params=pltpu.CompilerParams(
-            collective_id=0, has_side_effects=True, vmem_limit_bytes=62 * 2**20
+            collective_id=0, has_side_effects=True, vmem_limit_bytes=48 * 2**20
         ),
         name="transform",
     )(source, table, order, periodic)
+    return pl.pallas_call(
+        place,
+        out_shape=jax.ShapeDtypeStruct((1, 2, half, wide), F32),
+        in_specs=[any_spec],
+        out_specs=any_spec,
+        scratch_shapes=[pltpu.SemaphoreType.DMA((wide // 128, 2))],
+        compiler_params=pltpu.CompilerParams(vmem_limit_bytes=4 * 2**20),
+        name="place",
+    )(pltpu.with_memory_space_constraint(tiles, pltpu.VMEM))
 
 
 def solution(mesh):

time: 217 us -> 208 us (0.959)
  local copies, waits for them, and re-layouts: 7.76 us -> 0 us
    unnamed x1 -> x0, local copies, waits for them, and re-layouts: 7.76 us -> none
    pallas_call x1 -> x2, Pallas kernels: 207 us -> 206 us  [the longest x1 203 us: local(): pl.pallas_call(kernel, out_shape=pltpu.VMEM((wide // 128, 2, half, 128),...]
where the time goes in v3:
time: 208 us; the launch traced here: 206 us
  Pallas kernels  206 us (99%)
    pallas_call x1, Pallas kernels, local(): pl.pallas_call(kernel, out_shape=pltpu.VMEM((wide // 128, 2, half, 128),...  203 us

profile of v3, /device:TPU:25, one launch (start us, length us, event | category | flops | bytes accessed | tf_op | source)
XLA Modules:
  0.0 206.0 jit_solution(14963730180388746105)
XLA Ops:
  0.0 202.6 %transform.1.tiles = f32[4,2,2048,128]{3,2,1,0:T(8,128)S(1)} custom-call(f32[16,256,512]{2,1,0:T(8,128)} %source.1, bf16[2,8,1024,512]{3,2,1,0:T(8,128)(2,1)} %constant.6.clone.span_table, bf16[2,512,512]{2,1,0:T(8,128)(2,1)} %constant.7.clone.order_table, bf16[8,1024,512]{2,1,0:T(8,128)(2,1)} %constant.8.clone.periodic_table), custom_call_target="tpu_custom_call" | custom-call | tf_op jit(solution)/shard_map/transform/pallas_call | solution.py:374
  202.7 3.4 %place.1 = f32[1,2,2048,512]{3,2,1,0:T(8,128)} custom-call(f32[4,2,2048,128]{3,2,1,0:T(8,128)S(1)} %transform.1.tiles), custom_call_target="tpu_custom_call" | custom-call | tf_op jit(solution)/shard_map/place/pallas_call | solution.py:401

commit v4 on v3

--- a/solution.py
+++ b/solution.py
@@ -13,6 +13,7 @@
 BF16 = jnp.bfloat16
 F32 = jnp.float32
 CHUNKS = 4
+PIECES = 16
 STEP = 41
 
 
@@ -142,6 +143,16 @@
     groups, planes, wide = got.shape[1], got.shape[2], got.shape[4]
     peers = groups * planes - 1
     last = CHUNKS - 1
+
+    def rows_for(group, c, start, size):
+        return source.at[pl.ds(start, size), pl.ds(pl.multiple_of(group * (CHUNKS * 8) + c * 8, 8), 8), :]
+
+    for c in range(CHUNKS):
+        pltpu.make_async_copy(rows_for(gz, c, 0, planes), got.at[c, gz], own_sem.at[c]).start()
+    table_copy = pltpu.make_async_copy(span_table, tables, table_sem.at[0])
+    order_copy = pltpu.make_async_copy(order_table, orders, table_sem.at[1])
+    table_copy.start()
+    order_copy.start()
     barrier = pltpu.get_barrier_semaphore()
 
     def greet_span(t, carry):
@@ -156,15 +167,14 @@
     lax.fori_loop(1, planes, greet_planes, 0)
     pl.semaphore_wait(barrier, groups + planes - 2)
 
-    def rows_for(group, c):
-        return source.at[:, pl.ds(pl.multiple_of(group * (CHUNKS * 8) + c * 8, 8), 8), :]
+    size = planes // PIECES
 
     def scatter(i, carry):
-        c, t = i // (groups - 1), i % (groups - 1) + 1
+        c, start, t = i // (groups - 1) // PIECES, (i // (groups - 1)) % PIECES * size, i % (groups - 1) + 1
         to = ((z + t // 2) % 4) * 2 + (gz + t) % 2
         pltpu.make_async_remote_copy(
-            src_ref=rows_for(to, c),
-            dst_ref=got.at[c, gz],
+            src_ref=rows_for(to, c, start, size),
+            dst_ref=got.at[c, gz, pl.ds(start, size)],
             send_sem=send1,
             recv_sem=recv1.at[c],
             device_id=(to, gx),
@@ -172,13 +182,7 @@
         ).start()
         return carry
 
-    lax.fori_loop(0, CHUNKS * (groups - 1), scatter, 0)
-    for c in range(CHUNKS):
-        pltpu.make_async_copy(rows_for(gz, c), got.at[c, gz], own_sem.at[c]).start()
-    table_copy = pltpu.make_async_copy(span_table, tables, table_sem.at[0])
-    order_copy = pltpu.make_async_copy(order_table, orders, table_sem.at[1])
-    table_copy.start()
-    order_copy.start()
+    lax.fori_loop(0, CHUNKS * PIECES * (groups - 1), scatter, 0)
     table_copy.wait()
     order_copy.wait()
 
@@ -186,7 +190,7 @@
 
     def take(c):
         pltpu.make_async_copy(got.at[c, 0 : groups - 1], got.at[c, 0 : groups - 1], recv1.at[c]).wait()
-        pltpu.make_async_copy(rows_for(gz, c), got.at[c, gz], own_sem.at[c]).wait()
+        pltpu.make_async_copy(rows_for(gz, c, 0, planes), got.at[c, gz], own_sem.at[c]).wait()
 
     def span_chunk(c):
         def first(i, inner):
@@ -259,16 +263,13 @@
         take(c)
         span_chunk(c)
         mine(c, every).start()
+        send(c, c, every)
         return carry
 
     lax.fori_loop(0, last, early, 0)
-    send(0, 0, every)
     take(last)
-    send(1, 1, every)
     span_chunk(last)
     mine(last, every).start()
-    for c in range(2, last):
-        send(c, c, every)
     for h in range(2):
         send(last, last + h, sides[h])
 

time: 208 us -> 201 us (0.966)
  Pallas kernels: 206 us -> 200 us
    pallas_call x1, Pallas kernels: 203 us -> 197 us  [local(): pl.pallas_call(kernel, out_shape=pltpu.VMEM((wide // 128, 2, half, 128),...]
where the time goes in v4:
time: 201 us; the launch traced here: 200 us
  Pallas kernels  200 us (100%)
    pallas_call x1, Pallas kernels, local(): pl.pallas_call(kernel, out_shape=pltpu.VMEM((wide // 128, 2, half, 128),...  197 us

profile of v4, /device:TPU:25, one launch (start us, length us, event | category | flops | bytes accessed | tf_op | source)
XLA Modules:
  0.0 200.2 jit_solution(3480728386244987480)
XLA Ops:
  0.0 196.8 %transform.1.tiles = f32[4,2,2048,128]{3,2,1,0:T(8,128)S(1)} custom-call(f32[16,256,512]{2,1,0:T(8,128)} %source.1, bf16[2,8,1024,512]{3,2,1,0:T(8,128)(2,1)} %constant.6.clone.span_table, bf16[2,512,512]{2,1,0:T(8,128)(2,1)} %constant.7.clone.order_table, bf16[8,1024,512]{2,1,0:T(8,128)(2,1)} %constant.8.clone.periodic_table), custom_call_target="tpu_custom_call" | custom-call | tf_op jit(solution)/shard_map/transform/pallas_call | solution.py:375
  196.8 3.4 %place.1 = f32[1,2,2048,512]{3,2,1,0:T(8,128)} custom-call(f32[4,2,2048,128]{3,2,1,0:T(8,128)S(1)} %transform.1.tiles), custom_call_target="tpu_custom_call" | custom-call | tf_op jit(solution)/shard_map/place/pallas_call | solution.py:402

commit v5 on v4

--- a/solution.py
+++ b/solution.py
@@ -14,7 +14,8 @@
 F32 = jnp.float32
 CHUNKS = 4
 PIECES = 16
-STEP = 41
+STEP = 33
+BASE = 64
 
 
 def halves(table):
@@ -147,24 +148,24 @@
     def rows_for(group, c, start, size):
         return source.at[pl.ds(start, size), pl.ds(pl.multiple_of(group * (CHUNKS * 8) + c * 8, 8), 8), :]
 
+    barrier = pltpu.get_barrier_semaphore()
+
+    def greet_span(t, carry):
+        pl.semaphore_signal(barrier, inc=1, device_id=((gz + t) % groups, gx), device_id_type=MESH)
+        return carry
+
+    def greet_planes(t, carry):
+        pl.semaphore_signal(barrier, inc=1, device_id=(gz, (gx + t) % planes), device_id_type=MESH)
+        return carry
+
+    lax.fori_loop(1, groups, greet_span, 0)
+    lax.fori_loop(1, planes, greet_planes, 0)
     for c in range(CHUNKS):
         pltpu.make_async_copy(rows_for(gz, c, 0, planes), got.at[c, gz], own_sem.at[c]).start()
     table_copy = pltpu.make_async_copy(span_table, tables, table_sem.at[0])
     order_copy = pltpu.make_async_copy(order_table, orders, table_sem.at[1])
     table_copy.start()
     order_copy.start()
-    barrier = pltpu.get_barrier_semaphore()
-
-    def greet_span(t, carry):
-        pl.semaphore_signal(barrier, inc=1, device_id=((gz + t) % groups, gx), device_id_type=MESH)
-        return carry
-
-    def greet_planes(t, carry):
-        pl.semaphore_signal(barrier, inc=1, device_id=(gz, (gx + t) % planes), device_id_type=MESH)
-        return carry
-
-    lax.fori_loop(1, groups, greet_span, 0)
-    lax.fori_loop(1, planes, greet_planes, 0)
     pl.semaphore_wait(barrier, groups + planes - 2)
 
     size = planes // PIECES
@@ -182,7 +183,8 @@
         ).start()
         return carry
 
-    lax.fori_loop(0, CHUNKS * PIECES * (groups - 1), scatter, 0)
+    each_chunk = PIECES * (groups - 1)
+    lax.fori_loop(0, 2 * each_chunk, scatter, 0)
     table_copy.wait()
     order_copy.wait()
 
@@ -239,7 +241,7 @@
 
     def send(c, slot, lanes):
         def one(t, inner):
-            o = (t * STEP) % peers + 1
+            o = (t * STEP + BASE) % peers + 1
             to_x = (x_ring + (o // 8) % 4) % 4
             to_gz = ((z + o // 32) % 4) * 2 + to_x // 2
             to_gx = (to_x % 2) * 8 + ((y + (o // 2) % 4) % 4) * 2 + (core + o) % 2
@@ -261,6 +263,11 @@
 
     def early(c, carry):
         take(c)
+
+        @pl.when(c + 2 < CHUNKS)
+        def _():
+            lax.fori_loop((c + 2) * each_chunk, (c + 3) * each_chunk, scatter, 0)
+
         span_chunk(c)
         mine(c, every).start()
         send(c, c, every)
@@ -326,9 +333,9 @@
             table_high, table_low = tables[0, p, 0:wide, main:wide], tables[0, p, wide : 2 * wide, main:wide]
             line_high, line_low = tables[1, p, main:wide, sides[h]], tables[1, p, wide + main : 2 * wide, sides[h]]
             value = dot(
-                jnp.concatenate([table_high, table_high], axis=1),
-                jnp.concatenate([line_high, line_low], axis=0),
-            ) + dot(table_low, line_high)
+                jnp.concatenate([table_high, table_high, table_low], axis=1),
+                jnp.concatenate([line_high, line_low, line_high], axis=0),
+            )
             for which in range(2):
                 residue = (p, planes - p)[which] if p else (0, pairs)[which]
                 for part in range(2):

time: 201 us -> 200 us (level)
    pallas_call x1, Pallas kernels: 197 us -> 195 us  [local(): pl.pallas_call(kernel, out_shape=pltpu.VMEM((wide // 128, 2, half, 128),...]
where the time goes in v5:
time: 200 us; the launch traced here: 198 us
  Pallas kernels  198 us (99%)
    pallas_call x1, Pallas kernels, local(): pl.pallas_call(kernel, out_shape=pltpu.VMEM((wide // 128, 2, half, 128),...  195 us

profile of v5, /device:TPU:25, one launch (start us, length us, event | category | flops | bytes accessed | tf_op | source)
XLA Modules:
  0.0 198.0 jit_solution(3096555886534096376)
XLA Ops:
  0.0 194.6 %transform.1.tiles = f32[4,2,2048,128]{3,2,1,0:T(8,128)S(1)} custom-call(f32[16,256,512]{2,1,0:T(8,128)} %source.1, bf16[2,8,1024,512]{3,2,1,0:T(8,128)(2,1)} %constant.6.clone.span_table, bf16[2,512,512]{2,1,0:T(8,128)(2,1)} %constant.7.clone.order_table, bf16[8,1024,512]{2,1,0:T(8,128)(2,1)} %constant.8.clone.periodic_table), custom_call_target="tpu_custom_call" | custom-call | tf_op jit(solution)/shard_map/transform/pallas_call | solution.py:382
  194.6 3.4 %place.1 = f32[1,2,2048,512]{3,2,1,0:T(8,128)} custom-call(f32[4,2,2048,128]{3,2,1,0:T(8,128)S(1)} %transform.1.tiles), custom_call_target="tpu_custom_call" | custom-call | tf_op jit(solution)/shard_map/place/pallas_call | solution.py:409

commit v6 on v5

--- a/solution.py
+++ b/solution.py
@@ -13,7 +13,7 @@
 BF16 = jnp.bfloat16
 F32 = jnp.float32
 CHUNKS = 4
-PIECES = 16
+PIECES = 8
 STEP = 33
 BASE = 64
 

time: 200 us -> 200 us (level)
  no operation moved by 1% of the time
where the time goes in v6:
time: 200 us; the launch traced here: 198 us
  Pallas kernels  198 us (99%)
    pallas_call x1, Pallas kernels, local(): pl.pallas_call(kernel, out_shape=pltpu.VMEM((wide // 128, 2, half, 128),...  195 us

profile of v6, /device:TPU:25, one launch (start us, length us, event | category | flops | bytes accessed | tf_op | source)
XLA Modules:
  0.0 198.0 jit_solution(10196112031394564113)
XLA Ops:
  0.0 194.6 %transform.1.tiles = f32[4,2,2048,128]{3,2,1,0:T(8,128)S(1)} custom-call(f32[16,256,512]{2,1,0:T(8,128)} %source.1, bf16[2,8,1024,512]{3,2,1,0:T(8,128)(2,1)} %constant.6.clone.span_table, bf16[2,512,512]{2,1,0:T(8,128)(2,1)} %constant.7.clone.order_table, bf16[8,1024,512]{2,1,0:T(8,128)(2,1)} %constant.8.clone.periodic_table), custom_call_target="tpu_custom_call" | custom-call | tf_op jit(solution)/shard_map/transform/pallas_call | solution.py:382
  194.6 3.4 %place.1 = f32[1,2,2048,512]{3,2,1,0:T(8,128)} custom-call(f32[4,2,2048,128]{3,2,1,0:T(8,128)S(1)} %transform.1.tiles), custom_call_target="tpu_custom_call" | custom-call | tf_op jit(solution)/shard_map/place/pallas_call | solution.py:409
